TPU v7x, 256 devices: a whole 4x4x8 slice. The times are simulated.
256 devices in a mesh: rep: 64 (over z_hi, y, x), tp: 4 (over z_lo, core).
Axes of the slice: x: 4, y: 4, z: 8 (z_hi: 4, z_lo: 2; z = z_hi * 2 + z_lo), core: 2. Of those that a mesh axis runs over, the one named last changes fastest.
Arguments:
- attn_out: bfloat16 [64, 512, 2048], P('rep', None, 'tp'), may hold values from -6 to 6
- proj_weight: bfloat16 [64, 2048, 4608], P('rep', 'tp'), may hold values from -0.125 to 0.125
- norm_gain: float32 [64, 4608], P('rep'), may hold values from 0.5 to 1.5
- cotangent: bfloat16 [64, 512, 4608], P('rep', 'tp'), may hold values from -3 to 3
- coeffs: float32 [64, 4, 48, 64, 64], P('rep', 'tp'), may hold values from -192 to 192
- tile_ids: int32 [64, 4, 48], P('rep', 'tp'), may hold values from 0 to 511, as said below
- tiles: float32 [4, 512, 64, 64], P('tp', 'rep'), may hold values from -6 to 6
- momentum: float32 [4, 512, 64, 64], P('tp', 'rep'), may hold values from -3 to 3
Outputs:
- weight_grad: bfloat16 [64, 2048, 4608], P('rep', 'tp')
- input_grad: bfloat16 [64, 512, 2048], P('rep', None, 'tp')
- tiles_new: float32 [4, 512, 64, 64], P('tp', 'rep')
- momentum_new: float32 [4, 512, 64, 64], P('tp', 'rep')
Inputs may be any that keep to these rules, and one draw needn't show every extreme that they name: The owner of tile i is i // 8. For each replica r and group t, at most 2 entries of tile_ids[r, t, :] name tiles of one owner; in every group some owner is named exactly 2 times by every replica.
All inputs are finite; a program needn't handle non-finite values.
Results may differ from a plain program's by a relative error of at most 0.0095.
Values may be sent and summed in bfloat16 or wider, within the bound.
A program may use at most 128 MiB of HBM per device.

v0:
```python
import jax
import jax.numpy as jnp
from jax import lax
from jax.sharding import PartitionSpec as P

eps = 1e-06
outer_rate = 0.7
momentum_decay = 0.9


def norm_back(projected, upstream, norm_scale):
    inverse_rms = lax.rsqrt(jnp.mean(projected * projected, axis=-1, keepdims=True) + eps)
    normed = projected * inverse_rms
    scaled = upstream * norm_scale
    return (
        inverse_rms * (scaled - normed * jnp.mean(scaled * normed, axis=-1, keepdims=True))
    ).astype(jnp.bfloat16)


def dct_basis(size):
    freq = jnp.arange(size, dtype=jnp.float32)[:, None]
    place = jnp.arange(size, dtype=jnp.float32)[None, :]
    scales = jnp.where(freq == 0, jnp.sqrt(1.0 / size), jnp.sqrt(2.0 / size))
    return scales * jnp.cos(jnp.pi * (2.0 * place + 1.0) * freq / (2.0 * size))


def decode(coef_tiles, basis):
    right = jnp.einsum("jkl,lb->jkb", coef_tiles, basis, precision=lax.Precision.HIGHEST)
    return jnp.einsum("ka,jkb->jab", basis, right, precision=lax.Precision.HIGHEST)


def shards(attn_out, proj_weight, norm_gain, cotangent, coeffs, tile_ids, tiles, momentum):
    attended = attn_out[0]
    weights = proj_weight[0]
    norm_scale = norm_gain[0]
    rows_in = attended
    own_proj = lax.psum_scatter(
        jnp.dot(rows_in, weights, preferred_element_type=jnp.float32).astype(jnp.bfloat16),
        "tp",
        scatter_dimension=0,
        tiled=True,
    ).astype(jnp.float32)
    own_grad = norm_back(own_proj, cotangent[0].astype(jnp.float32), norm_scale)
    piece = lax.all_gather(own_grad, "tp", axis=0, tiled=True)
    rows_in = attended
    grad_sum = lax.dot_general(
        rows_in, piece, (((0,), (0,)), ((), ())), preferred_element_type=jnp.float32
    )
    back_rows = lax.dot_general(
        piece, weights, (((1,), (1,)), ((), ())), preferred_element_type=jnp.float32
    )
    grad_sum, back_all = (grad_sum, back_rows)
    weight_grad = grad_sum.astype(jnp.bfloat16)[None]
    input_grad = back_all.astype(jnp.bfloat16)[None]
    owned = tiles.shape[1]
    side = tiles.shape[2]
    tile_area = side * side
    replicas = lax.axis_size("rep")
    kept_flat = coeffs[0, 0].reshape(-1, tile_area)
    tile_names = tile_ids[0, 0]
    row_names = jnp.arange(lax.axis_size("rep") * owned, dtype=jnp.int32)
    onehot = (row_names[:, None] == tile_names[None, :]).astype(jnp.float32)
    coef_sums = lax.psum_scatter(
        jnp.dot(onehot, kept_flat, precision=lax.Precision.HIGHEST),
        "rep",
        scatter_dimension=0,
        tiled=True,
    )
    decoded = decode(coef_sums.reshape(owned, side, side), dct_basis(side)) / replicas
    momentum_new = momentum_decay * momentum[0] + decoded
    tiles_new = tiles[0] - outer_rate * (decoded + momentum_decay * momentum_new)
    return (weight_grad, input_grad, tiles_new[None], momentum_new[None])


def solution(mesh):
    in_specs = (
        P("rep", None, "tp"),
        P("rep", "tp", None),
        P("rep", None),
        P("rep", "tp", None),
        P("rep", "tp", None, None, None),
        P("rep", "tp", None),
        P("tp", "rep", None, None),
        P("tp", "rep", None, None),
    )
    out_specs = (
        P("rep", "tp", None),
        P("rep", None, "tp"),
        P("tp", "rep", None, None),
        P("tp", "rep", None, None),
    )
    return jax.shard_map(shards, mesh=mesh, in_specs=in_specs, out_specs=out_specs, check_vma=False)
```

profile of v0, /device:TPU:0, one launch (start us, length us, event | category | flops | bytes accessed | tf_op | source)
XLA Modules:
  0.0 526.1 jit_solution(3646842157126613007)
XLA Ops:
  8.0 0.0 copy-start
  8.0 0.0 reduce-scatter.3.cloned.1.call-start
  8.1 1.0 copy-done
  9.0 6.5 %convolution_convert_fusion.1 = bf16[512,4608]{1,0:T(8,128)(2,1)} fusion(bf16[1,512,4608]{2,1,0:T(8,128)(2,1)} %param.9, bf16[1,512,512]{2,1,0:T(8,128)(2,1)S(1)} %copy-done), kind=kOutput, calls=%fused_computation.1 | convolution fusion | flops 2418278400 | bytes 9961472 | tf_op jit(solution)/shard_map/dot_general | solution.py:38
  15.6 0.0 copy-start.6
  15.6 0.0 copy-start.2
  15.6 0.0 reduce-scatter.3.cloned.1.call-update
  15.6 0.0 all-gather.2.cloned.1.call-start
  15.7 0.6 copy-done.6
  16.4 52.9 %reduce-scatter.3.cloned.1.call-done = bf16[128,4608]{1,0:T(8,128)(2,1)} async-done(((bf16[512,4608]{1,0:T(8,128)(2,1)}), bf16[128,4608]{1,0:T(8,128)(2,1)}) %reduce-scatter.3.cloned.1.call-update) | async-done | bytes 1179664 | tf_op jit(solution)/shard_map/reduce_scatter | solution.py:37
  69.3 0.0 copy-start.1
  69.3 1.7 fusion.10
  71.0 0.0 copy-done.2
  71.0 1.9 fusion.6
  72.8 0.0 copy-done.1
  72.9 0.0 copy-start.3
  72.9 1.7 fusion.9
  74.5 0.0 copy-start.7
  74.5 0.0 all-gather.2.cloned.1.call-update
  74.6 0.0 reduce-scatter.5.cloned.1.call-start
  74.6 0.0 copy-done.3
  74.6 0.5 reshape_squeeze.3
  75.1 0.1 copy-done.7
  75.2 5.7 %fusion.21 = f32[512,4096]{1,0:T(8,128)} fusion(f32[48,4096]{1,0:T(8,128)S(1)} %reshape_squeeze.3, s32[48]{0:T(128)S(1)} %bitcast.57), kind=kOutput, calls=%fused_computation.26 | convolution fusion | flops 1207984128 | bytes 9175232 | tf_op jit(solution)/shard_map/dot_general | solution.py:64
  80.9 0.0 copy-start.4
  80.9 0.0 copy-start.5
  80.9 0.0 reduce-scatter.5.cloned.1.call-update
  80.9 0.9 copy-done.4
  81.8 0.1 copy.12
  81.9 0.0 copy-done.5
  82.0 0.1 copy.13
  82.1 52.9 %all-gather.2.cloned.1.call-done = bf16[512,4608]{1,0:T(8,128)(2,1)} async-done(((bf16[128,4608]{1,0:T(8,128)(2,1)}), bf16[512,4608]{1,0:T(8,128)(2,1)}) %all-gather.2.cloned.1.call-update) | async-done | bytes 4718608 | tf_op jit(solution)/shard_map/all_gather | solution.py:44
  135.0 6.6 %fusion = bf16[1,512,4608]{1,2,0:T(8,128)(2,1)} fusion(bf16[512,4608]{1,0:T(8,128)(2,1)} %all-gather.2.cloned.1.call-done, bf16[1,512,512]{2,1,0:T(8,128)(2,1)S(1)} %copy-done), kind=kOutput, calls=%fused_computation.2 | convolution fusion | flops 2418278400 | bytes 9961472 | tf_op jit(solution)/shard_map/dot_general | solution.py:46
  141.7 6.6 %copy.14 = bf16[1,512,4608]{2,1,0:T(8,128)(2,1)} copy(bf16[1,512,4608]{1,2,0:T(8,128)(2,1)} %fusion) | data formatting | bytes 9437184
  148.3 7.2 %fusion.14 = bf16[1,512,512]{2,1,0:T(8,128)(2,1)} fusion(bf16[512,4608]{1,0:T(8,128)(2,1)} %all-gather.2.cloned.1.call-done, bf16[1,512,4608]{2,1,0:T(8,128)(2,1)} %param.9), kind=kOutput, calls=%fused_computation.17 | convolution fusion | flops 2416181248 | bytes 9961472 | tf_op jit(solution)/shard_map/dot_general | solution.py:49
  155.5 359.0 %reduce-scatter.5.cloned.1.call-done = f32[8,4096]{1,0:T(8,128)} async-done(((f32[512,4096]{1,0:T(8,128)}), f32[8,4096]{1,0:T(8,128)}) %reduce-scatter.5.cloned.1.call-update) | async-done | bytes 131088 | tf_op jit(solution)/shard_map/reduce_scatter | solution.py:63
  514.5 1.0 reshape.44
  515.5 1.0 fusion.25
  516.5 0.5 fusion.22
  517.0 0.8 copy.15
  517.9 0.8 copy.16
  (4 shorter events, 0.1 us)
Async XLA Ops:
  8.0 1.0 copy-start
  8.0 61.3 %reduce-scatter.3.cloned.1.call-start = ((), (), s32[]{:S(2)}) async-start(), calls=%async_computation.2 | async-start | bytes 5898240 | tf_op jit(solution)/shard_map/reduce_scatter | solution.py:37
  15.6 0.7 copy-start.6
  15.6 55.4 %copy-start.2 = (bf16[1,128,4608]{2,1,0:T(8,128)(2,1)S(1)}, bf16[1,128,4608]{2,1,0:T(8,128)(2,1)}, u32[]{:S(2)}) copy-start(bf16[1,128,4608]{2,1,0:T(8,128)(2,1)} %param.11) | copy-start | bytes 3538948
  15.6 119.4 %all-gather.2.cloned.1.call-start = ((), (), s32[]{:S(2)}) async-start(), calls=%async_computation.3 | async-start | bytes 5898240 | tf_op jit(solution)/shard_map/all_gather | solution.py:44
  69.3 3.6 copy-start.1
  72.9 1.8 copy-start.3
  74.5 0.7 copy-start.7
  74.6 439.9 %reduce-scatter.5.cloned.1.call-start = ((), (), s32[]{:S(2)}) async-start(), calls=%async_computation.4 | async-start | bytes 8519680 | tf_op jit(solution)/shard_map/reduce_scatter | solution.py:63
  80.9 0.9 copy-start.4
  80.9 1.1 copy-start.5
Sparse Core Ops, SparseCore 0:
  15.7 53.4 reduce-scatter.2
  74.7 60.3 all-gather.1
Sparse Core Ops, SparseCore 1:
  81.0 433.5 reduce-scatter.4
where the time goes:
time: 527 us; the launch traced here: 526 us
  waiting for transfers between devices  465 us (88%)
  matrix products  27.6 us (5%)
  between operations  15.6 us (3%)
  local copies, waits for them, and re-layouts  12.7 us (2%)
  other arithmetic  5.3 us (1%)
    reduce_scatter x1, waiting for transfers between devices, shards(): lax.psum_scatter(jnp.dot(onehot, kept_flat, precision=lax.Precision.HIGHE...  359 us
    all_gather x1, waiting for transfers between devices, shards(): piece = lax.all_gather(own_grad, 'tp', axis=0, tiled=True)  52.9 us
    reduce_scatter x1, waiting for transfers between devices, shards(): lax.psum_scatter(jnp.dot(rows_in, weights, preferred_element_type=jnp.flo...  52.9 us
    unnamed x21, local copies, waits for them, and re-layouts  11.2 us
  transfers between devices with their start and end apart: 3, of which 3 were waited for; matrix products, arithmetic and copies ran while one was open for 5% of the time, Pallas kernels for 0%

commit v1 on v0

v1 whole, which is shorter than its diff:
```python
import jax
import jax.numpy as jnp
import numpy as np
from jax import lax
from jax.experimental import pallas as pl
from jax.experimental.pallas import tpu as pltpu
from jax.sharding import PartitionSpec as P

eps = 1e-06
outer_rate = 0.7
momentum_decay = 0.9
MESH = pl.DeviceIdType.MESH
PLANES = 4
PARTS = 4
ROW_CHUNKS = (32, 32, 32, 32)
HEAD = 16


def dct_basis(size):
    freq = np.arange(size, dtype=np.float64)[:, None]
    place = np.arange(size, dtype=np.float64)[None, :]
    scales = np.where(freq == 0, np.sqrt(1.0 / size), np.sqrt(2.0 / size))
    return (scales * np.cos(np.pi * (2.0 * place + 1.0) * freq / (2.0 * size))).astype(np.float32)


def owner_table(names, owners, owned):
    entry = jnp.arange(names.shape[0], dtype=jnp.int32)[None, :]
    match = (names // owned)[None, :] == jnp.arange(owners, dtype=jnp.int32)[:, None]
    place = (names % owned)[None, :]
    first = jnp.min(jnp.where(match, entry, names.shape[0]), axis=1)
    last = jnp.max(jnp.where(match, entry, -1), axis=1)
    first_place = jnp.max(jnp.where(match & (entry == first[:, None]), place, -1), axis=1)
    last_place = jnp.max(
        jnp.where(match & (entry == last[:, None]) & (entry > first[:, None]), place, -1), axis=1
    )
    first = jnp.where(first_place >= 0, first, 0)
    last = jnp.maximum(last, 0)
    return jnp.stack([first, last, first_place, last_place])


def step_kernel(
    table, attn_hbm, w_hbm, gain_hbm, ct_hbm, coef_hbm, tiles_hbm, mom_hbm, left_hbm, right_hbm,
    wg_hbm, ig_hbm, tiles_out, mom_out,
    attn, attn_t, w, gain, ct, coef, tiles, mom, left, right,
    part, sib_part, pair_sum, far_sum, proj, grad, acc, wg, ig,
    pack, packs_in, sums, sums_out, sums_in, tiles_new, mom_new,
    in_sem, w_sem, attn_sem, out_sem, wg_sem, ig_sem,
    core_s, core_r, z_s, z_r, gz_s, gz_r, gc_s, gc_r, gf_s, gf_r,
    pa_s, pa_r, pb_s, pb_r,
):
    n_rep = lax.axis_size("rep")
    planes = PLANES
    n_xy = n_rep // planes
    rep, tp = lax.axis_index("rep"), lax.axis_index("tp")
    xy, zh = lax.rem(rep, n_xy), lax.div(rep, n_xy)
    core, zl = lax.rem(tp, 2), lax.div(tp, 2)
    sib = zl * 2 + 1 - core
    far = (1 - zl) * 2 + core
    diag = (1 - zl) * 2 + 1 - core
    order = (tp, far, sib, diag)
    depth = w.shape[0]
    width = w.shape[1]
    rows = ct.shape[0]
    tile_w = w_sem_width(width)
    n_w = width // tile_w
    side = coef.shape[1]
    chunks = []
    off = 0
    for size in ROW_CHUNKS:
        chunks.append((off, size))
        off += size
    f32, bf16 = jnp.float32, jnp.bfloat16

    def xy_peer(d):
        return zh * n_xy + lax.rem(xy + d, n_xy)

    def zh_peer(e):
        return lax.rem(zh + e, planes) * n_xy + xy

    loads = []
    for j, (o, s) in enumerate(chunks):
        for p in range(PARTS):
            start = pl.multiple_of(order[p] * rows + o, 16)
            copy = pltpu.make_async_copy(
                attn_hbm.at[pl.ds(start, s)],
                attn.at[pl.ds(4 * o + p * s, s)],
                attn_sem.at[j * PARTS + p],
            )
            copy.start()
            loads.append(copy)
    w_loads = []
    for n in range(n_w):
        cols = pl.ds(n * tile_w, tile_w)
        copy = pltpu.make_async_copy(w_hbm.at[:, cols], w.at[:, cols], w_sem.at[n])
        copy.start()
        w_loads.append(copy)
    others = []
    for i, (src, dst) in enumerate(
        ((coef_hbm, coef), (ct_hbm, ct), (gain_hbm, gain), (tiles_hbm, tiles), (mom_hbm, mom),
         (left_hbm, left), (right_hbm, right))
    ):
        copy = pltpu.make_async_copy(src, dst, in_sem.at[i])
        copy.start()
        others.append(copy)
    coef_load, ct_load, gain_load, tiles_load, mom_load, left_load, right_load = others

    barrier = pltpu.get_barrier_semaphore()
    pl.semaphore_signal(barrier, inc=1, device_id=(rep, sib), device_id_type=MESH)
    pl.semaphore_signal(barrier, inc=1, device_id=(rep, far), device_id_type=MESH)

    @pl.loop(1, n_xy)
    def _(d):
        pl.semaphore_signal(barrier, inc=1, device_id=(xy_peer(d), tp), device_id_type=MESH)

    @pl.loop(1, planes)
    def _(e):
        pl.semaphore_signal(barrier, inc=1, device_id=(zh_peer(e), tp), device_id_type=MESH)

    def partial_chunk(j):
        o, s = chunks[j]
        block = attn[4 * o:4 * o + 4 * s, :]

        @pl.loop(0, n_w)
        def _(n):
            cols = pl.ds(pl.multiple_of(n * tile_w, tile_w), tile_w)
            if j == 0:
                pltpu.make_async_copy(w_hbm.at[:, cols], w.at[:, cols], w_sem.at[n]).wait()
            part[4 * o:4 * o + 4 * s, cols] = jnp.dot(
                block, w[:, cols], preferred_element_type=f32
            ).astype(bf16)

    def remote(src, dst, send, recv, rep_to, tp_to):
        return pltpu.make_async_remote_copy(
            src_ref=src, dst_ref=dst, send_sem=send, recv_sem=recv,
            device_id=(rep_to, tp_to), device_id_type=MESH,
        )

    def core_copy(j):
        o, s = chunks[j]
        return remote(
            part.at[pl.ds(4 * o + 2 * s, 2 * s)], sib_part.at[pl.ds(2 * o, 2 * s)],
            core_s.at[j], core_r.at[j], rep, sib,
        )

    def z_copy(j):
        o, s = chunks[j]
        return remote(
            pair_sum.at[pl.ds(o, s)], far_sum.at[pl.ds(o, s)], z_s.at[j], z_r.at[j], rep, far
        )

    def grad_far(j):
        o, s = chunks[j]
        return remote(
            grad.at[pl.ds(4 * o, s)], grad.at[pl.ds(4 * o + s, s)], gz_s.at[j], gz_r.at[j], rep, far
        )

    def grad_core(j):
        o, s = chunks[j]
        return remote(
            grad.at[pl.ds(4 * o, s)], grad.at[pl.ds(4 * o + 2 * s, s)],
            gc_s.at[j], gc_r.at[j], rep, sib,
        )

    def grad_forward(j):
        o, s = chunks[j]
        return remote(
            grad.at[pl.ds(4 * o + s, s)], grad.at[pl.ds(4 * o + 3 * s, s)],
            gf_s.at[j], gf_r.at[j], rep, sib,
        )

    def pair_chunk(j):
        o, s = chunks[j]
        core_copy(j).wait_recv()

        @pl.loop(0, n_w)
        def _(n):
            cols = pl.ds(pl.multiple_of(n * tile_w, tile_w), tile_w)
            pair_sum[o:o + s, cols] = (
                part[4 * o + s:4 * o + 2 * s, cols].astype(f32)
                + sib_part[2 * o + s:2 * o + 2 * s, cols].astype(f32)
            ).astype(bf16)

        z_copy(j).start()

    def fold(block):
        total = block[:, 0:128]
        for k in range(1, block.shape[1] // 128):
            total = total + block[:, k * 128:(k + 1) * 128]
        return total

    def norm_chunk(j):
        o, s = chunks[j]
        z_copy(j).wait_recv()

        def stats(n, carry):
            square, cross = carry
            cols = pl.ds(pl.multiple_of(n * tile_w, tile_w), tile_w)
            p = (
                part[4 * o:4 * o + s, cols].astype(f32)
                + sib_part[2 * o:2 * o + s, cols].astype(f32)
                + far_sum[o:o + s, cols].astype(f32)
            )
            proj[0:s, cols] = p
            scaled = ct[o:o + s, cols].astype(f32) * gain[:, cols]
            return square + fold(p * p), cross + fold(scaled * p)

        zero = jnp.zeros((s, 128), f32)
        square, cross = lax.fori_loop(0, n_w, stats, (zero, zero))
        inverse = lax.rsqrt(jnp.sum(square, axis=1, keepdims=True) / width + eps)
        slope = jnp.sum(cross, axis=1, keepdims=True) / width * inverse * inverse

        @pl.loop(0, n_w)
        def _(n):
            cols = pl.ds(pl.multiple_of(n * tile_w, tile_w), tile_w)
            scaled = ct[o:o + s, cols].astype(f32) * gain[:, cols]
            grad[4 * o:4 * o + s, cols] = (inverse * (scaled - proj[0:s, cols] * slope)).astype(bf16)

        grad_far(j).start()
        grad_core(j).start()

    lane = lax.broadcasted_iota(jnp.int32, (HEAD, 2 * side), 1)
    line = lax.broadcasted_iota(jnp.int32, (HEAD, 2 * side), 0)

    def pack_for(d, dst):
        to = lax.rem(xy + d, n_xy)
        head = jnp.full((HEAD, 2 * side), -1.0, f32)
        for h in range(planes):
            o = h * n_xy + to
            both = jnp.concatenate([coef[table[0, o]], coef[table[1, o]]], axis=1)
            dst[h * side:(h + 1) * side, :] = both.astype(bf16)
            place = jnp.where(lane < side, table[2, o].astype(f32), table[3, o].astype(f32))
            head = jnp.where(line == h, place, head)
        dst[planes * side:planes * side + HEAD, :] = head.astype(bf16)

    def pack_copy(d):
        return remote(
            pack.at[d], packs_in.at[d], pa_s.at[d], pa_r.at[d], xy_peer(d), tp
        )

    def pack_all():
        coef_load.wait()
        pack_for(0, packs_in.at[0])

        @pl.loop(1, n_xy)
        def _(d):
            pack_for(d, pack.at[d])
            pack_copy(d).start()

    half = lax.broadcasted_iota(jnp.int32, (1, 2 * side), 1)
    half = jnp.where(half < side, 0.0, 1.0).astype(f32)
    pairs = 4

    def sums_copy(e):
        return remote(
            sums_out.at[lax.rem(zh + e, planes)], sums_in.at[e], pb_s.at[e], pb_r.at[e],
            zh_peer(e), tp,
        )

    def sum_packs():
        @pl.loop(1, n_xy)
        def _(d):
            pack_copy(d).wait_recv()

        for h in range(planes):
            def add(d, totals):
                block = packs_in[d, h * side:(h + 1) * side, :].astype(f32)
                turned = pltpu.roll(block, side, 1)
                head = packs_in[d, planes * side:planes * side + HEAD, :].astype(f32)[h:h + 1, :]
                here = head - half
                there = pltpu.roll(jnp.broadcast_to(head, (8, 2 * side)), side, 1)[0:1, :] - half
                return tuple(
                    total
                    + jnp.where(here == 2.0 * p, block, 0.0)
                    + jnp.where(there == 2.0 * p, turned, 0.0)
                    for p, total in enumerate(totals)
                )

            zero = jnp.zeros((side, 2 * side), f32)
            totals = lax.fori_loop(0, n_xy, add, (zero,) * pairs)
            for p in range(pairs):
                sums[h, p * side:(p + 1) * side, :] = totals[p]
                sums_out[h, p * side:(p + 1) * side, :] = totals[p].astype(bf16)

        @pl.loop(1, planes)
        def _(e):
            sums_copy(e).start()

    def outer_step():
        @pl.loop(1, planes)
        def _(e):
            sums_copy(e).wait_recv()

        total = sums[zh]
        for e in range(1, planes):
            total = total + sums_in[e].astype(f32)
        for copy in (tiles_load, mom_load, left_load, right_load):
            copy.wait()
        wide = jnp.dot(total, right[...], precision=lax.Precision.HIGHEST)
        for p in range(pairs):
            decoded = jnp.dot(
                left[...], wide[p * side:(p + 1) * side, :], precision=lax.Precision.HIGHEST
            ) / n_rep
            for i in range(2):
                one = decoded[:, i * side:(i + 1) * side]
                fresh = momentum_decay * mom[2 * p + i] + one
                mom_new[2 * p + i] = fresh
                tiles_new[2 * p + i] = tiles[2 * p + i] - outer_rate * (one + momentum_decay * fresh)
        pltpu.make_async_copy(tiles_new, tiles_out, out_sem.at[0]).start()
        pltpu.make_async_copy(mom_new, mom_out, out_sem.at[1]).start()

    def ig_copies(j):
        o, s = chunks[j]
        out = []
        for p in range(PARTS):
            start = pl.multiple_of(order[p] * rows + o, 16)
            out.append(pltpu.make_async_copy(
                ig.at[pl.ds(4 * o + p * s, s)], ig_hbm.at[pl.ds(start, s)],
                ig_sem.at[j * PARTS + p],
            ))
        return out

    def input_chunk(j):
        o, s = chunks[j]
        ig[4 * o:4 * o + 4 * s, :] = lax.dot_general(
            grad[4 * o:4 * o + 4 * s, :], w[...], (((1,), (1,)), ((), ())),
            preferred_element_type=f32,
        ).astype(bf16)
        for copy in ig_copies(j):
            copy.start()

    def wg_copy(n):
        cols = pl.ds(pl.multiple_of(n * tile_w, tile_w), tile_w)
        return pltpu.make_async_copy(wg.at[:, cols], wg_hbm.at[:, cols], wg_sem.at[n])

    last = len(chunks) - 1
    early = 4 * chunks[last][0]

    for copy in loads:
        copy.wait()
    for j in range(last + 1):
        partial_chunk(j)
        if j == 0:
            pl.semaphore_wait(barrier, n_xy + planes)
        core_copy(j).start()
        if j == 0:
            pack_all()
        pair_chunk(j)
    attn_t[...] = attn[...].T
    ct_load.wait()
    gain_load.wait()
    norm_chunk(0)
    sum_packs()
    for j in range(1, last + 1):
        norm_chunk(j)
    outer_step()

    def arrived(j):
        grad_far(j).wait_recv()
        grad_forward(j).start()
        grad_core(j).wait_recv()

    for j in range(last):
        arrived(j)
        grad_forward(j).wait_recv()
        input_chunk(j)

    @pl.loop(0, n_w)
    def _(n):
        cols = pl.ds(pl.multiple_of(n * tile_w, tile_w), tile_w)
        acc[:, cols] = jnp.dot(
            attn_t[:, 0:early], grad[0:early, cols], preferred_element_type=f32
        )

    arrived(last)
    grad_forward(last).wait_recv()

    @pl.loop(0, n_w)
    def _(n):
        cols = pl.ds(pl.multiple_of(n * tile_w, tile_w), tile_w)
        wg[:, cols] = (
            acc[:, cols]
            + jnp.dot(attn_t[:, early:], grad[early:, cols], preferred_element_type=f32)
        ).astype(bf16)
        wg_copy(n).start()

    input_chunk(last)

    for j in range(last + 1):
        core_copy(j).wait_send()
        z_copy(j).wait_send()
        grad_far(j).wait_send()
        grad_core(j).wait_send()
        grad_forward(j).wait_send()
        for copy in ig_copies(j):
            copy.wait()

    @pl.loop(1, n_xy)
    def _(d):
        pack_copy(d).wait_send()

    @pl.loop(1, planes)
    def _(e):
        sums_copy(e).wait_send()

    pltpu.make_async_copy(tiles_new, tiles_out, out_sem.at[0]).wait()
    pltpu.make_async_copy(mom_new, mom_out, out_sem.at[1]).wait()

    @pl.loop(0, n_w)
    def _(n):
        wg_copy(n).wait()


def w_sem_width(width):
    return 512 if width % 512 == 0 else 256


def shards(attn_out, proj_weight, norm_gain, cotangent, coeffs, tile_ids, tiles, momentum):
    n_rep = lax.axis_size("rep")
    attended, weights, upstream = attn_out[0], proj_weight[0], cotangent[0]
    owned, side = tiles.shape[1], tiles.shape[2]
    tokens, depth = attended.shape
    width = weights.shape[1]
    rows = upstream.shape[0]
    n_w = width // w_sem_width(width)
    n_chunks = len(ROW_CHUNKS)
    n_xy = n_rep // PLANES
    kept = coeffs.shape[2]
    table = owner_table(tile_ids[0, 0], n_rep, owned)
    basis = dct_basis(side)
    right = np.zeros((2 * side, 2 * side), np.float32)
    right[:side, :side] = basis
    right[side:, side:] = basis
    f32, bf16 = jnp.float32, jnp.bfloat16
    dma = pltpu.SemaphoreType.DMA
    any_spec = pl.BlockSpec(memory_space=pl.ANY)
    message = PLANES * side + HEAD
    outs = pl.pallas_call(
        step_kernel,
        out_shape=(
            jax.ShapeDtypeStruct((depth, width), bf16),
            jax.ShapeDtypeStruct((tokens, depth), bf16),
            jax.ShapeDtypeStruct((owned, side, side), f32),
            jax.ShapeDtypeStruct((owned, side, side), f32),
        ),
        in_specs=[pl.BlockSpec(memory_space=pltpu.SMEM)] + [any_spec] * 9,
        out_specs=(any_spec,) * 4,
        scratch_shapes=[
            pltpu.VMEM((tokens, depth), bf16),
            pltpu.VMEM((depth, tokens), bf16),
            pltpu.VMEM((depth, width), bf16),
            pltpu.VMEM((1, width), f32),
            pltpu.VMEM((rows, width), bf16),
            pltpu.VMEM((kept, side, side), f32),
            pltpu.VMEM((owned, side, side), f32),
            pltpu.VMEM((owned, side, side), f32),
            pltpu.VMEM((side, side), f32),
            pltpu.VMEM((2 * side, 2 * side), f32),
            pltpu.VMEM((tokens, width), bf16),
            pltpu.VMEM((2 * rows, width), bf16),
            pltpu.VMEM((rows, width), bf16),
            pltpu.VMEM((rows, width), bf16),
            pltpu.VMEM((max(ROW_CHUNKS), width), f32),
            pltpu.VMEM((tokens, width), bf16),
            pltpu.VMEM((depth, width), f32),
            pltpu.VMEM((depth, width), bf16),
            pltpu.VMEM((tokens, depth), bf16),
            pltpu.VMEM((n_xy, message, 2 * side), bf16),
            pltpu.VMEM((n_xy, message, 2 * side), bf16),
            pltpu.VMEM((PLANES, owned // 2 * side, 2 * side), f32),
            pltpu.VMEM((PLANES, owned // 2 * side, 2 * side), bf16),
            pltpu.VMEM((PLANES, owned // 2 * side, 2 * side), bf16),
            pltpu.VMEM((owned, side, side), f32),
            pltpu.VMEM((owned, side, side), f32),
            dma((7,)), dma((n_w,)), dma((n_chunks * PARTS,)), dma((2,)), dma((n_w,)),
            dma((n_chunks * PARTS,)),
            *[dma((n_chunks,)) for _ in range(10)],
            dma((n_xy,)), dma((n_xy,)), dma((PLANES,)), dma((PLANES,)),
        ],
        compiler_params=pltpu.CompilerParams(
            collective_id=0, has_side_effects=True, vmem_limit_bytes=60 * 1024 * 1024
        ),
        cost_estimate=pl.CostEstimate(
            flops=6 * tokens * depth * width, bytes_accessed=16_000_000, transcendentals=0
        ),
    )(
        table, attended, weights, norm_gain, upstream, coeffs[0, 0], tiles[0], momentum[0],
        jnp.asarray(np.ascontiguousarray(basis.T)), jnp.asarray(right),
    )
    weight_grad, input_grad, tiles_new, momentum_new = outs
    return (weight_grad[None], input_grad[None], tiles_new[None], momentum_new[None])


def solution(mesh):
    in_specs = (
        P("rep", None, "tp"),
        P("rep", "tp", None),
        P("rep", None),
        P("rep", "tp", None),
        P("rep", "tp", None, None, None),
        P("rep", "tp", None),
        P("tp", "rep", None, None),
        P("tp", "rep", None, None),
    )
    out_specs = (
        P("rep", "tp", None),
        P("rep", None, "tp"),
        P("tp", "rep", None, None),
        P("tp", "rep", None, None),
    )
    return jax.shard_map(shards, mesh=mesh, in_specs=in_specs, out_specs=out_specs, check_vma=False)
```

time: 527 us -> 86.7 us (0.16)
  the two profiles are of different devices: /device:TPU:0 before, /device:TPU:1 now
where the time goes in v1:
time: 86.7 us; the launch traced here: 86.6 us
  Pallas kernels  77.3 us (89%)
  local copies, waits for them, and re-layouts  7.12 us (8%)
  other arithmetic  1.45 us (2%)
    pallas_call x1, Pallas kernels, shards(): pl.pallas_call(step_kernel, out_shape=(jax.ShapeDtypeStruct((depth, width...  77.3 us
    unnamed x10, local copies, waits for them, and re-layouts  7.12 us

profile of v1, /device:TPU:1, one launch (start us, length us, event | category | flops | bytes accessed | tf_op | source)
XLA Modules:
  0.0 86.6 jit_solution(11519546479706375854)
XLA Ops:
  0.6 0.7 and_select_fusion.1
  1.3 0.1 select_reduce_fusion.3
  1.4 0.1 select_reduce_fusion.2
  1.5 0.6 pad_add_fusion.table
  2.1 77.3 %shard_map.129 = (bf16[512,4608]{1,0:T(8,128)(2,1)}, bf16[512,512]{1,0:T(8,128)(2,1)}, f32[8,64,64]{2,1,0:T(8,128)}, f32[8,64,64]{2,1,0:T(8,128)}) custom-call(s32[4,64]{1,0:T(4,128)} %pad_add_fusion.table, bf16[512,512]{1,0:T(8,128)(2,1)} %bitcast.41, bf16[512,4608]{1,0:T(8,128)(2,1)} %bitcast.38, f32[1,4608]{1,0:T(1,128)} %gain_hbm.1, ...), custom_call_target="tpu_custom_call" | custom-call | flops 7247757312 | bytes 16000000 | tf_op jit(solution)/shard_map/pallas_call | solution.py:437
  79.4 0.0 copy-start
  79.5 0.0 copy-start.2
  79.5 0.0 copy-start.1
  79.5 4.9 %copy.18 = bf16[1,512,4608]{2,1,0:T(8,128)(2,1)} copy(bf16[1,512,4608]{2,1,0:T(8,128)(2,1)} %bitcast.32) | data formatting | bytes 9437184
  84.4 0.0 copy-done
  84.4 0.8 copy.19
  85.2 0.0 copy-done.2
  85.2 0.7 copy.20
  85.9 0.0 copy-done.1
  85.9 0.7 copy.21
  (2 shorter events, 0.0 us)
Async XLA Ops:
  79.4 4.9 %copy-start = (bf16[512,512]{1,0:T(8,128)(2,1)S(1)}, bf16[512,512]{1,0:T(8,128)(2,1)}, u32[]{:S(2)}) copy-start(bf16[512,512]{1,0:T(8,128)(2,1)} %get-tuple-element.9) | copy-start | bytes 1572868
  79.5 5.7 %copy-start.2 = (f32[8,64,64]{2,1,0:T(8,128)S(1)}, f32[8,64,64]{2,1,0:T(8,128)}, u32[]{:S(2)}) copy-start(f32[8,64,64]{2,1,0:T(8,128)} %get-tuple-element.10) | copy-start | bytes 393220
  79.5 6.4 %copy-start.1 = (f32[8,64,64]{2,1,0:T(8,128)S(1)}, f32[8,64,64]{2,1,0:T(8,128)}, u32[]{:S(2)}) copy-start(f32[8,64,64]{2,1,0:T(8,128)} %get-tuple-element.11) | copy-start | bytes 393220

commit v2 on v0

v2 whole, which is shorter than its diff:
```python
import jax
import jax.numpy as jnp
import numpy as np
from jax import lax
from jax.experimental import pallas as pl
from jax.experimental.pallas import tpu as pltpu
from jax.sharding import PartitionSpec as P

eps = 1e-06
outer_rate = 0.7
momentum_decay = 0.9
MESH = pl.DeviceIdType.MESH
PLANES = 4
PARTS = 4
HALVES = 2
FIRST = 4
STEP_VMEM = 55 * 1024 * 1024
WRITE_FROM = pl.ANY
HEAD = 16


def dct_basis(size):
    freq = np.arange(size, dtype=np.float64)[:, None]
    place = np.arange(size, dtype=np.float64)[None, :]
    scales = np.where(freq == 0, np.sqrt(1.0 / size), np.sqrt(2.0 / size))
    return (scales * np.cos(np.pi * (2.0 * place + 1.0) * freq / (2.0 * size))).astype(np.float32)


def owner_table(names, owners, owned):
    kept = names.shape[0]
    match = (names // owned)[None, :] == jnp.arange(owners, dtype=jnp.int32)[:, None]
    key = (jnp.arange(kept, dtype=jnp.int32) * owned + names % owned)[None, :]
    least = jnp.min(jnp.where(match, key, kept * owned - 1), axis=1)
    return jnp.stack([least, jnp.max(jnp.where(match, key, -1), axis=1)])


def step_kernel(
    table, attn_hbm, w_hbm, gain_hbm, ct_hbm, coef_hbm, tiles_hbm, mom_hbm, left_hbm, right_hbm,
    wg, ig, tiles_new, mom_new,
    attn, attn_t, w, gain, ct, coef, tiles, mom, left, right,
    part, sib_part, pair_sum, far_sum, proj, grad, acc, ig_acc,
    pack, packs_in, sums, near_out, near_in, last_out, last_in,
    in_sem, w_sem, attn_sem,
    core_s, core_r, z_s, z_r, gz_s, gz_r, gc_s, gc_r, gf_s, gf_r,
    pa_s, pa_r, pb_s, pb_r,
):
    n_rep = lax.axis_size("rep")
    planes = PLANES
    n_xy = n_rep // planes
    rep, tp = lax.axis_index("rep"), lax.axis_index("tp")
    xy, zh = lax.rem(rep, n_xy), lax.div(rep, n_xy)
    core, zl = lax.rem(tp, 2), lax.div(tp, 2)
    sib = zl * 2 + 1 - core
    far = (1 - zl) * 2 + core
    diag = (1 - zl) * 2 + 1 - core
    order = (tp, far, sib, diag)
    near = zh + 1 - 2 * lax.rem(zh, 2)
    next_near = planes - 1 - zh
    width = w.shape[1]
    rows = ct.shape[0]
    s = rows // HALVES
    tile_w = tile_width(width)
    n_w = width // tile_w
    side = coef.shape[1]
    owned = tiles.shape[0]
    pairs = owned // 2
    kept = coef.shape[0]
    f32, bf16 = jnp.float32, jnp.bfloat16

    def cols(n):
        return pl.ds(pl.multiple_of(n * tile_w, tile_w), tile_w)

    def xy_peer(d):
        return zh * n_xy + lax.rem(xy + d, n_xy)

    def plane_peer(z):
        return z * n_xy + xy

    loads = []
    for h in range(HALVES):
        for p in range(PARTS):
            start = pl.multiple_of(order[p] * rows + h * s, 16)
            loads.append(pltpu.make_async_copy(
                attn_hbm.at[pl.ds(start, s)],
                attn.at[pl.ds((h * PARTS + p) * s, s)],
                attn_sem.at[h * PARTS + p],
            ))
    for copy in loads:
        copy.start()

    def w_load(n):
        return pltpu.make_async_copy(w_hbm.at[:, cols(n)], w.at[:, cols(n)], w_sem.at[n])

    @pl.loop(0, n_w)
    def _(n):
        w_load(n).start()

    others = [
        pltpu.make_async_copy(src, dst, in_sem.at[i])
        for i, (src, dst) in enumerate(
            ((coef_hbm, coef), (ct_hbm, ct), (gain_hbm, gain), (tiles_hbm, tiles), (mom_hbm, mom),
             (left_hbm, left), (right_hbm, right))
        )
    ]
    coef_load, ct_load, gain_load, tiles_load, mom_load, left_load, right_load = others
    for copy in others:
        copy.start()

    barrier = pltpu.get_barrier_semaphore()
    for rep_to, tp_to in (
        (rep, sib), (rep, far), (plane_peer(near), tp), (plane_peer(next_near), tp)
    ):
        pl.semaphore_signal(barrier, inc=1, device_id=(rep_to, tp_to), device_id_type=MESH)

    @pl.loop(1, n_xy)
    def _(d):
        pl.semaphore_signal(barrier, inc=1, device_id=(xy_peer(d), tp), device_id_type=MESH)

    def remote(src, dst, send, recv, rep_to, tp_to):
        return pltpu.make_async_remote_copy(
            src_ref=src, dst_ref=dst, send_sem=send, recv_sem=recv,
            device_id=(rep_to, tp_to), device_id_type=MESH,
        )

    def core_copy(h, n):
        i = h * n_w + n
        return remote(
            part.at[pl.ds((h * PARTS + 2) * s, 2 * s), cols(n)],
            sib_part.at[pl.ds(h * 2 * s, 2 * s), cols(n)],
            core_s.at[i], core_r.at[i], rep, sib,
        )

    def z_copy(h, n):
        i = h * n_w + n
        here = pl.ds(h * s, s)
        return remote(
            pair_sum.at[here, cols(n)], far_sum.at[here, cols(n)], z_s.at[i], z_r.at[i], rep, far
        )

    def grad_copy(h, n, place, to, send, recv, target):
        i = h * n_w + n
        return remote(
            grad.at[pl.ds((h * PARTS + place) * s, s), cols(n)],
            grad.at[pl.ds((h * PARTS + to) * s, s), cols(n)],
            send.at[i], recv.at[i], rep, target,
        )

    def grad_far(h, n):
        return grad_copy(h, n, 0, 1, gz_s, gz_r, far)

    def grad_core(h, n):
        return grad_copy(h, n, 0, 2, gc_s, gc_r, sib)

    def grad_forward(h, n):
        return grad_copy(h, n, 1, 3, gf_s, gf_r, sib)

    def partial_tile(h, n):
        here = slice(h * PARTS * s, (h + 1) * PARTS * s)
        part[here, cols(n)] = jnp.dot(
            attn[here, :], w[:, cols(n)], preferred_element_type=f32
        ).astype(bf16)
        core_copy(h, n).start()

    def pair_tile(h, n):
        core_copy(h, n).wait_recv()
        base = h * PARTS * s + s
        pair_sum[h * s:h * s + s, cols(n)] = (
            part[base:base + s, cols(n)].astype(f32)
            + sib_part[h * 2 * s + s:(h + 1) * 2 * s, cols(n)].astype(f32)
        ).astype(bf16)
        z_copy(h, n).start()

    def fold(block):
        total = block[:, 0:128]
        for k in range(1, block.shape[1] // 128):
            total = total + block[:, k * 128:(k + 1) * 128]
        return total

    def norm_half(h):
        here = slice(h * s, h * s + s)
        base = h * PARTS * s

        def stats(n, carry):
            square, cross = carry
            z_copy(h, n).wait_recv()
            p = (
                part[base:base + s, cols(n)].astype(f32)
                + sib_part[h * 2 * s:h * 2 * s + s, cols(n)].astype(f32)
                + far_sum[here, cols(n)].astype(f32)
            )
            proj[:, cols(n)] = p
            scaled = ct[here, cols(n)].astype(f32) * gain[:, cols(n)]
            return square + fold(p * p), cross + fold(scaled * p)

        zero = jnp.zeros((s, 128), f32)
        square, cross = lax.fori_loop(0, n_w, stats, (zero, zero))
        inverse = lax.rsqrt(jnp.sum(square, axis=1, keepdims=True) / width + eps)
        slope = jnp.sum(cross, axis=1, keepdims=True) / width * inverse * inverse

        @pl.loop(0, n_w)
        def _(n):
            scaled = ct[here, cols(n)].astype(f32) * gain[:, cols(n)]
            grad[base:base + s, cols(n)] = (
                inverse * (scaled - proj[:, cols(n)] * slope)
            ).astype(bf16)
            grad_core(h, n).start()

    def send_far(h, low, high):
        @pl.loop(low, high)
        def _(n):
            grad_far(h, n).start()

    lane = lax.broadcasted_iota(jnp.int32, (HEAD, 2 * side), 1)
    line = lax.broadcasted_iota(jnp.int32, (HEAD, 2 * side), 0)

    def pack_for(d, dst):
        to = lax.rem(xy + d, n_xy)
        head = jnp.full((HEAD, 2 * side), -1.0, f32)
        for h in range(planes):
            o = h * n_xy + to
            least, most = table[0, o], table[1, o]
            one, two = least // owned, jnp.maximum(most, 0) // owned
            both = jnp.concatenate([coef[one], coef[two]], axis=1)
            dst[h * side:(h + 1) * side, :] = both.astype(bf16)
            one_place = jnp.where(most >= 0, least - one * owned, -1)
            two_place = jnp.where(most > least, most - two * owned, -1)
            place = jnp.where(lane < side, one_place.astype(f32), two_place.astype(f32))
            head = jnp.where(line == h, place, head)
        dst[planes * side:planes * side + HEAD, :] = head.astype(bf16)

    def pack_copy(d):
        return remote(pack.at[d], packs_in.at[d], pa_s.at[d], pa_r.at[d], xy_peer(d), tp)

    each = -(-n_xy // (n_w - 1))

    def pack_some(n):
        for i in range(each):
            d = (n - 1) * each + 1 + i

            @pl.when(d < n_xy)
            def _():
                pack_for(d, pack.at[d])
                pack_copy(d).start()

            @pl.when(d == n_xy)
            def _():
                pack_for(n_xy, packs_in.at[0])

    half = lax.broadcasted_iota(jnp.int32, (1, 2 * side), 1)
    half = jnp.where(half < side, 0.0, 1.0).astype(f32)

    def near_copy():
        return remote(near_out, near_in, pb_s.at[0], pb_r.at[0], plane_peer(near), tp)

    def last_copy():
        return remote(last_out, last_in, pb_s.at[1], pb_r.at[1], plane_peer(next_near), tp)

    def sum_packs():
        @pl.loop(1, n_xy)
        def _(d):
            pack_copy(d).wait_recv()

        for h in range(planes):
            def add(d, totals):
                block = packs_in[d, h * side:(h + 1) * side, :].astype(f32)
                turned = pltpu.roll(block, side, 1)
                head = packs_in[d, planes * side:planes * side + HEAD, :].astype(f32)[h:h + 1, :]
                here = head - half
                there = pltpu.roll(jnp.broadcast_to(head, (8, 2 * side)), side, 1)[0:1, :] - half
                return tuple(
                    total
                    + jnp.where(here == 2.0 * p, block, 0.0)
                    + jnp.where(there == 2.0 * p, turned, 0.0)
                    for p, total in enumerate(totals)
                )

            zero = jnp.zeros((side, 2 * side), f32)
            totals = lax.fori_loop(0, n_xy, add, (zero,) * pairs)
            for p in range(pairs):
                sums[h, p * side:(p + 1) * side, :] = totals[p]
        near_out[0] = sums[near].astype(bf16)
        near_out[1] = sums[planes - 1 - near].astype(bf16)
        near_copy().start()

    def pass_on():
        near_copy().wait_recv()
        last_out[...] = (sums[next_near] + near_in[1].astype(f32)).astype(bf16)
        last_copy().start()

    def outer_step():
        last_copy().wait_recv()
        total = sums[zh] + near_in[0].astype(f32) + last_in[...].astype(f32)
        for copy in (tiles_load, mom_load, left_load, right_load):
            copy.wait()
        wide = jnp.dot(total, right[...], precision=lax.Precision.HIGHEST)
        for p in range(pairs):
            decoded = jnp.dot(
                left[...], wide[p * side:(p + 1) * side, :], precision=lax.Precision.HIGHEST
            ) / n_rep
            for i in range(2):
                one = decoded[:, i * side:(i + 1) * side]
                fresh = momentum_decay * mom[2 * p + i] + one
                mom_new[2 * p + i] = fresh
                tiles_new[2 * p + i] = tiles[2 * p + i] - outer_rate * (one + momentum_decay * fresh)

    def arrive(h, n):
        grad_far(h, n).wait_recv()
        grad_forward(h, n).start()

    def use_tile(h, n):
        grad_core(h, n).wait_recv()
        grad_forward(h, n).wait_recv()
        here = slice(h * PARTS * s, (h + 1) * PARTS * s)
        block = grad[here, cols(n)]
        product = jnp.dot(attn_t[:, here], block, preferred_element_type=f32)
        if h == 0:
            acc[:, cols(n)] = product
        elif h < HALVES - 1:
            acc[:, cols(n)] += product
        else:
            wg[:, cols(n)] = (acc[:, cols(n)] + product).astype(bf16)
        ig_acc[here, :] += lax.dot_general(
            block, w[:, cols(n)], (((1,), (1,)), ((), ())), preferred_element_type=f32
        )

    def use_half(h, low, high):
        if low == 0:
            arrive(h, 0)

        @pl.loop(low, high)
        def _(n):
            @pl.when(n + 1 < n_w)
            def _():
                arrive(h, n + 1)

            use_tile(h, n)

    def finish_input(h):
        for p in range(PARTS):
            start = pl.multiple_of(order[p] * rows + h * s, 16)
            base = (h * PARTS + p) * s
            ig[pl.ds(start, s), :] = ig_acc[base:base + s, :].astype(bf16)

    for copy in loads:
        copy.wait()
    for h in range(HALVES):
        if h == 0:
            w_load(0).wait()
            pl.semaphore_wait(barrier, n_xy + 3)
        partial_tile(h, 0)

        @pl.loop(1, n_w)
        def _(n):
            if h == 0:
                w_load(n).wait()
            partial_tile(h, n)
            pair_tile(h, n - 1)
            if h == 0:
                @pl.when(n == 1)
                def _():
                    coef_load.wait()

                pack_some(n)

        pair_tile(h, n_w - 1)
    attn_t[...] = attn[...].T
    ig_acc[...] = jnp.zeros_like(ig_acc)
    ct_load.wait()
    gain_load.wait()
    first = min(FIRST, n_w - 1)
    norm_half(0)
    send_far(0, 0, first)
    sum_packs()
    send_far(0, first, n_w)
    norm_half(1)
    use_half(0, 0, first - 1)
    pass_on()
    send_far(1, 0, n_w)
    use_half(0, first - 1, n_w)
    finish_input(0)
    outer_step()
    use_half(1, 0, n_w)
    finish_input(1)

    for h in range(HALVES):
        @pl.loop(0, n_w)
        def _(n):
            core_copy(h, n).wait_send()
            z_copy(h, n).wait_send()
            grad_far(h, n).wait_send()
            grad_core(h, n).wait_send()
            grad_forward(h, n).wait_send()

    @pl.loop(1, n_xy)
    def _(d):
        pack_copy(d).wait_send()

    near_copy().wait_send()
    last_copy().wait_send()


def write_kernel(*refs):
    sources, targets, sem = refs[:4], refs[4:8], refs[8]
    pieces = 8
    step = sources[0].shape[0] // pieces
    copies = [
        pltpu.make_async_copy(
            sources[0].at[pl.ds(i * step, step)], targets[0].at[pl.ds(i * step, step)], sem.at[i]
        )
        for i in range(pieces)
    ]
    copies += [
        pltpu.make_async_copy(sources[i], targets[i], sem.at[pieces + i - 1]) for i in range(1, 4)
    ]
    for copy in copies:
        copy.start()
    for copy in copies:
        copy.wait()


def tile_width(width):
    return 512


def shards(attn_out, proj_weight, norm_gain, cotangent, coeffs, tile_ids, tiles, momentum):
    n_rep = lax.axis_size("rep")
    attended, weights, upstream = attn_out[0], proj_weight[0], cotangent[0]
    owned, side = tiles.shape[1], tiles.shape[2]
    tokens, depth = attended.shape
    width = weights.shape[1]
    rows = upstream.shape[0]
    n_w = width // tile_width(width)
    n_xy = n_rep // PLANES
    kept = coeffs.shape[2]
    table = owner_table(tile_ids[0, 0], n_rep, owned)
    basis = dct_basis(side)
    right = np.zeros((2 * side, 2 * side), np.float32)
    right[:side, :side] = basis
    right[side:, side:] = basis
    f32, bf16 = jnp.float32, jnp.bfloat16
    dma = pltpu.SemaphoreType.DMA
    any_spec = pl.BlockSpec(memory_space=pl.ANY)
    message = PLANES * side + HEAD
    summed = owned // 2 * side
    results = (
        ((depth, width), bf16),
        ((tokens, depth), bf16),
        ((owned, side, side), f32),
        ((owned, side, side), f32),
    )
    operands = (
        attended, weights, norm_gain, upstream, coeffs[0, 0], tiles[0], momentum[0],
        jnp.asarray(np.ascontiguousarray(basis.T)), jnp.asarray(right),
    )
    held = pl.pallas_call(
        step_kernel,
        out_shape=tuple(pltpu.VMEM(shape, dtype) for shape, dtype in results),
        in_specs=[pl.BlockSpec(memory_space=pltpu.SMEM)] + [any_spec] * len(operands),
        out_specs=(pl.BlockSpec(memory_space=pltpu.VMEM),) * 4,
        scratch_shapes=[
            pltpu.VMEM((tokens, depth), bf16),
            pltpu.VMEM((depth, tokens), bf16),
            pltpu.VMEM((depth, width), bf16),
            pltpu.VMEM((1, width), f32),
            pltpu.VMEM((rows, width), bf16),
            pltpu.VMEM((kept, side, side), f32),
            pltpu.VMEM((owned, side, side), f32),
            pltpu.VMEM((owned, side, side), f32),
            pltpu.VMEM((side, side), f32),
            pltpu.VMEM((2 * side, 2 * side), f32),
            pltpu.VMEM((tokens, width), bf16),
            pltpu.VMEM((2 * rows, width), bf16),
            pltpu.VMEM((rows, width), bf16),
            pltpu.VMEM((rows, width), bf16),
            pltpu.VMEM((rows // HALVES, width), f32),
            pltpu.VMEM((tokens, width), bf16),
            pltpu.VMEM((depth, width), f32),
            pltpu.VMEM((tokens, depth), f32),
            pltpu.VMEM((n_xy, message, 2 * side), bf16),
            pltpu.VMEM((n_xy, message, 2 * side), bf16),
            pltpu.VMEM((PLANES, summed, 2 * side), f32),
            pltpu.VMEM((2, summed, 2 * side), bf16),
            pltpu.VMEM((2, summed, 2 * side), bf16),
            pltpu.VMEM((summed, 2 * side), bf16),
            pltpu.VMEM((summed, 2 * side), bf16),
            dma((7,)), dma((n_w,)), dma((HALVES * PARTS,)),
            *[dma((HALVES * n_w,)) for _ in range(10)],
            dma((n_xy,)), dma((n_xy,)), dma((2,)), dma((2,)),
        ],
        compiler_params=pltpu.CompilerParams(
            collective_id=0, has_side_effects=True, vmem_limit_bytes=STEP_VMEM
        ),
        cost_estimate=pl.CostEstimate(
            flops=6 * tokens * depth * width, bytes_accessed=16_000_000, transcendentals=0
        ),
    )(table, *operands)
    outs = pl.pallas_call(
        write_kernel,
        out_shape=tuple(jax.ShapeDtypeStruct(shape, dtype) for shape, dtype in results),
        in_specs=[pl.BlockSpec(memory_space=WRITE_FROM)] * 4,
        out_specs=(any_spec,) * 4,
        scratch_shapes=[dma((11,))],
        compiler_params=pltpu.CompilerParams(vmem_limit_bytes=4 * 1024 * 1024),
    )(*held)
    return tuple(out[None] for out in outs)


def solution(mesh):
    in_specs = (
        P("rep", None, "tp"),
        P("rep", "tp", None),
        P("rep", None),
        P("rep", "tp", None),
        P("rep", "tp", None, None, None),
        P("rep", "tp", None),
        P("tp", "rep", None, None),
        P("tp", "rep", None, None),
    )
    out_specs = (
        P("rep", "tp", None),
        P("rep", None, "tp"),
        P("tp", "rep", None, None),
        P("tp", "rep", None, None),
    )
    return jax.shard_map(shards, mesh=mesh, in_specs=in_specs, out_specs=out_specs, check_vma=False)
```

time: 527 us -> 75.1 us (0.14)
  the two profiles are of different devices: /device:TPU:0 before, /device:TPU:1 now
where the time goes in v2:
time: 75.1 us; the launch traced here: 75 us
  Pallas kernels  73 us (97%)
  other arithmetic  1.34 us (2%)
    pallas_call x1, Pallas kernels, shards(): pl.pallas_call(step_kernel, out_shape=tuple((pltpu.VMEM(shape, dtype) for...  70.5 us
    pallas_call x1, Pallas kernels, shards(): pl.pallas_call(write_kernel, out_shape=tuple((jax.ShapeDtypeStruct(shape,...  2.59 us

profile of v2, /device:TPU:1, one launch (start us, length us, event | category | flops | bytes accessed | tf_op | source)
XLA Modules:
  0.0 75.0 jit_solution(11304264026074603077)
XLA Ops:
  0.6 0.7 and_select_fusion.1
  1.3 0.1 select_reduce_fusion.1
  1.4 0.6 pad_add_fusion.table
  2.0 70.5 %shard_map.129 = (bf16[512,4608]{1,0:T(8,128)(2,1)S(1)}, bf16[512,512]{1,0:T(8,128)(2,1)S(1)}, f32[8,64,64]{2,1,0:T(8,128)S(1)}, f32[8,64,64]{2,1,0:T(8,128)S(1)}) custom-call(s32[2,64]{1,0:T(2,128)} %pad_add_fusion.table, bf16[512,512]{1,0:T(8,128)(2,1)} %bitcast.33, bf16[512,4608]{1,0:T(8,128)(2,1)} %bitcast.29, f32[1,4608]{1,0:T(1,128)} %gain_hbm.1, ...), custom_call_target="tpu_custom_call" | custom-call | flops 7247757312 | bytes 16000000 | tf_op jit(solution)/shard_map/pallas_call | solution.py:455
  72.4 2.6 %shard_map.130 = (bf16[512,4608]{1,0:T(8,128)(2,1)}, bf16[512,512]{1,0:T(8,128)(2,1)}, f32[8,64,64]{2,1,0:T(8,128)}, f32[8,64,64]{2,1,0:T(8,128)}) custom-call(bf16[512,4608]{1,0:T(8,128)(2,1)S(1)} %get-tuple-element.12.refs_0_, bf16[512,512]{1,0:T(8,128)(2,1)S(1)} %get-tuple-element.13.refs_1_, f32[8,64,64]{2,1,0:T(8,128)S(1)} %get-tuple-element.14.refs_2_, ...), custom_call_target="tpu_custom_call" | custom-call | tf_op jit(solution)/shard_map/pallas_call | solution.py:497

commit v3 on v2

--- a/solution.py
+++ b/solution.py
@@ -13,7 +13,8 @@
 PLANES = 4
 PARTS = 4
 HALVES = 2
-FIRST = 4
+WINDOW = 5
+AHEAD = 3
 STEP_VMEM = 55 * 1024 * 1024
 WRITE_FROM = pl.ANY
 HEAD = 16
@@ -26,20 +27,13 @@
     return (scales * np.cos(np.pi * (2.0 * place + 1.0) * freq / (2.0 * size))).astype(np.float32)
 
 
-def owner_table(names, owners, owned):
-    kept = names.shape[0]
-    match = (names // owned)[None, :] == jnp.arange(owners, dtype=jnp.int32)[:, None]
-    key = (jnp.arange(kept, dtype=jnp.int32) * owned + names % owned)[None, :]
-    least = jnp.min(jnp.where(match, key, kept * owned - 1), axis=1)
-    return jnp.stack([least, jnp.max(jnp.where(match, key, -1), axis=1)])
-
-
 def step_kernel(
-    table, attn_hbm, w_hbm, gain_hbm, ct_hbm, coef_hbm, tiles_hbm, mom_hbm, left_hbm, right_hbm,
+    ids_hbm, attn_hbm, w_hbm, gain_hbm, ct_hbm, coef_hbm, tiles_hbm, mom_hbm, left_hbm, right_hbm,
     wg, ig, tiles_new, mom_new,
     attn, attn_t, w, gain, ct, coef, tiles, mom, left, right,
     part, sib_part, pair_sum, far_sum, proj, grad, acc, ig_acc,
     pack, packs_in, sums, near_out, near_in, last_out, last_in,
+    ids, keys, table,
     in_sem, w_sem, attn_sem,
     core_s, core_r, z_s, z_r, gz_s, gz_r, gc_s, gc_r, gf_s, gf_r,
     pa_s, pa_r, pb_s, pb_r,
@@ -91,20 +85,18 @@
     def w_load(n):
         return pltpu.make_async_copy(w_hbm.at[:, cols(n)], w.at[:, cols(n)], w_sem.at[n])
 
-    @pl.loop(0, n_w)
-    def _(n):
+    for n in range(min(AHEAD, n_w)):
         w_load(n).start()
 
     others = [
         pltpu.make_async_copy(src, dst, in_sem.at[i])
         for i, (src, dst) in enumerate(
-            ((coef_hbm, coef), (ct_hbm, ct), (gain_hbm, gain), (tiles_hbm, tiles), (mom_hbm, mom),
+            ((ids_hbm, ids), (coef_hbm, coef), (ct_hbm, ct), (gain_hbm, gain), (tiles_hbm, tiles), (mom_hbm, mom),
              (left_hbm, left), (right_hbm, right))
         )
     ]
-    coef_load, ct_load, gain_load, tiles_load, mom_load, left_load, right_load = others
-    for copy in others:
-        copy.start()
+    ids_load, coef_load, ct_load, gain_load, tiles_load, mom_load, left_load, right_load = others
+    ids_load.start()
 
     barrier = pltpu.get_barrier_semaphore()
     for rep_to, tp_to in (
@@ -121,6 +113,21 @@
             src_ref=src, dst_ref=dst, send_sem=send, recv_sem=recv,
             device_id=(rep_to, tp_to), device_id_type=MESH,
         )
+
+    def make_table():
+        entry = lax.broadcasted_iota(jnp.int32, (n_rep, kept), 1)
+        owner = lax.broadcasted_iota(jnp.int32, (n_rep, kept), 0)
+        names = jnp.broadcast_to(ids[...], (n_rep, kept))
+        match = (names >= owner * owned) & (names < owner * owned + owned)
+        key = entry * owned + names - owner * owned
+        least = jnp.min(jnp.where(match, key, kept * owned - 1), axis=1, keepdims=True)
+        most = jnp.max(jnp.where(match, key, -1), axis=1, keepdims=True)
+        lane = lax.broadcasted_iota(jnp.int32, keys.shape, 1)
+        keys[...] = jnp.where(lane == 0, least, most)
+        table_copy().start()
+
+    def table_copy():
+        return pltpu.make_async_copy(keys, table, in_sem.at[8])
 
     def core_copy(h, n):
         i = h * n_w + n
@@ -163,12 +170,33 @@
 
     def pair_tile(h, n):
         core_copy(h, n).wait_recv()
+        behind(h, n, lambda a, b: z_copy(a, b).wait_send())
         base = h * PARTS * s + s
         pair_sum[h * s:h * s + s, cols(n)] = (
             part[base:base + s, cols(n)].astype(f32)
             + sib_part[h * 2 * s + s:(h + 1) * 2 * s, cols(n)].astype(f32)
         ).astype(bf16)
         z_copy(h, n).start()
+
+    def behind(h, n, step):
+        @pl.when(n >= window)
+        def _():
+            step(h, n - window)
+
+        if h > 0:
+            @pl.when(n < window)
+            def _():
+                step(h - 1, n + n_w - window)
+
+    def ahead(h, n, step):
+        @pl.when(n + window < n_w)
+        def _():
+            step(h, n + window)
+
+        if h < HALVES - 1:
+            @pl.when(n + window >= n_w)
+            def _():
+                step(h + 1, n + window - n_w)
 
     def fold(block):
         total = block[:, 0:128]
@@ -218,7 +246,7 @@
         head = jnp.full((HEAD, 2 * side), -1.0, f32)
         for h in range(planes):
             o = h * n_xy + to
-            least, most = table[0, o], table[1, o]
+            least, most = table[o, 0], table[o, 1]
             one, two = least // owned, jnp.maximum(most, 0) // owned
             both = jnp.concatenate([coef[one], coef[two]], axis=1)
             dst[h * side:(h + 1) * side, :] = both.astype(bf16)
@@ -306,6 +334,8 @@
     def arrive(h, n):
         grad_far(h, n).wait_recv()
         grad_forward(h, n).start()
+        grad_far(h, n).wait_send()
+        ahead(h, n, lambda a, b: grad_far(a, b).start())
 
     def use_tile(h, n):
         grad_core(h, n).wait_recv()
@@ -341,23 +371,34 @@
             base = (h * PARTS + p) * s
             ig[pl.ds(start, s), :] = ig_acc[base:base + s, :].astype(bf16)
 
-    for copy in loads:
-        copy.wait()
+    window = min(WINDOW, n_w)
     for h in range(HALVES):
+        for copy in loads[h * PARTS:(h + 1) * PARTS]:
+            copy.wait()
         if h == 0:
             w_load(0).wait()
             pl.semaphore_wait(barrier, n_xy + 3)
         partial_tile(h, 0)
+        if h == 0:
+            for copy in others[1:]:
+                copy.start()
+            ids_load.wait()
+            make_table()
 
         @pl.loop(1, n_w)
         def _(n):
             if h == 0:
+                @pl.when(n + AHEAD - 1 < n_w)
+                def _():
+                    w_load(n + AHEAD - 1).start()
+
                 w_load(n).wait()
             partial_tile(h, n)
             pair_tile(h, n - 1)
             if h == 0:
                 @pl.when(n == 1)
                 def _():
+                    table_copy().wait()
                     coef_load.wait()
 
                 pack_some(n)
@@ -367,16 +408,13 @@
     ig_acc[...] = jnp.zeros_like(ig_acc)
     ct_load.wait()
     gain_load.wait()
-    first = min(FIRST, n_w - 1)
     norm_half(0)
-    send_far(0, 0, first)
+    send_far(0, 0, window)
     sum_packs()
-    send_far(0, first, n_w)
     norm_half(1)
-    use_half(0, 0, first - 1)
+    use_half(0, 0, window)
     pass_on()
-    send_far(1, 0, n_w)
-    use_half(0, first - 1, n_w)
+    use_half(0, window, n_w)
     finish_input(0)
     outer_step()
     use_half(1, 0, n_w)
@@ -386,10 +424,12 @@
         @pl.loop(0, n_w)
         def _(n):
             core_copy(h, n).wait_send()
-            z_copy(h, n).wait_send()
-            grad_far(h, n).wait_send()
             grad_core(h, n).wait_send()
             grad_forward(h, n).wait_send()
+
+    @pl.loop(n_w - window, n_w)
+    def _(n):
+        z_copy(HALVES - 1, n).wait_send()
 
     @pl.loop(1, n_xy)
     def _(d):
@@ -432,7 +472,6 @@
     n_w = width // tile_width(width)
     n_xy = n_rep // PLANES
     kept = coeffs.shape[2]
-    table = owner_table(tile_ids[0, 0], n_rep, owned)
     basis = dct_basis(side)
     right = np.zeros((2 * side, 2 * side), np.float32)
     right[:side, :side] = basis
@@ -449,13 +488,13 @@
         ((owned, side, side), f32),
     )
     operands = (
-        attended, weights, norm_gain, upstream, coeffs[0, 0], tiles[0], momentum[0],
+        tile_ids[0], attended, weights, norm_gain, upstream, coeffs[0, 0], tiles[0], momentum[0],
         jnp.asarray(np.ascontiguousarray(basis.T)), jnp.asarray(right),
     )
     held = pl.pallas_call(
         step_kernel,
         out_shape=tuple(pltpu.VMEM(shape, dtype) for shape, dtype in results),
-        in_specs=[pl.BlockSpec(memory_space=pltpu.SMEM)] + [any_spec] * len(operands),
+        in_specs=[any_spec] * len(operands),
         out_specs=(pl.BlockSpec(memory_space=pltpu.VMEM),) * 4,
         scratch_shapes=[
             pltpu.VMEM((tokens, depth), bf16),
@@ -483,7 +522,10 @@
             pltpu.VMEM((2, summed, 2 * side), bf16),
             pltpu.VMEM((summed, 2 * side), bf16),
             pltpu.VMEM((summed, 2 * side), bf16),
-            dma((7,)), dma((n_w,)), dma((HALVES * PARTS,)),
+            pltpu.VMEM((1, kept), jnp.int32),
+            pltpu.VMEM((n_rep, 128), jnp.int32),
+            pltpu.SMEM((n_rep, 128), jnp.int32),
+            dma((9,)), dma((n_w,)), dma((HALVES * PARTS,)),
             *[dma((HALVES * n_w,)) for _ in range(10)],
             dma((n_xy,)), dma((n_xy,)), dma((2,)), dma((2,)),
         ],
@@ -493,7 +535,7 @@
         cost_estimate=pl.CostEstimate(
             flops=6 * tokens * depth * width, bytes_accessed=16_000_000, transcendentals=0
         ),
-    )(table, *operands)
+    )(*operands)
     outs = pl.pallas_call(
         write_kernel,
         out_shape=tuple(jax.ShapeDtypeStruct(shape, dtype) for shape, dtype in results),

time: 75.1 us -> 74.8 us (level)
  other arithmetic: 1.34 us -> 0 us
  Pallas kernels: 73 us -> 74.1 us
    pallas_call x1, Pallas kernels: 70.5 us -> 71.5 us  [shards(): pl.pallas_call(step_kernel, out_shape=tuple((pltpu.VMEM(shape, dtype) for...]
where the time goes in v3:
time: 74.8 us; the launch traced here: 74.7 us
  Pallas kernels  74.1 us (99%)
    pallas_call x1, Pallas kernels, shards(): pl.pallas_call(step_kernel, out_shape=tuple((pltpu.VMEM(shape, dtype) for...  71.5 us
    pallas_call x1, Pallas kernels, shards(): pl.pallas_call(write_kernel, out_shape=tuple((jax.ShapeDtypeStruct(shape,...  2.59 us

profile of v3, /device:TPU:1, one launch (start us, length us, event | category | flops | bytes accessed | tf_op | source)
XLA Modules:
  0.0 74.7 jit_solution(3785663429848400383)
XLA Ops:
  0.6 71.5 %shard_map.129 = (bf16[512,4608]{1,0:T(8,128)(2,1)S(1)}, bf16[512,512]{1,0:T(8,128)(2,1)S(1)}, f32[8,64,64]{2,1,0:T(8,128)S(1)}, f32[8,64,64]{2,1,0:T(8,128)S(1)}) custom-call(s32[1,48]{1,0:T(1,128)} %bitcast.21, bf16[512,512]{1,0:T(8,128)(2,1)} %bitcast.15, bf16[512,4608]{1,0:T(8,128)(2,1)} %bitcast.11, f32[1,4608]{1,0:T(1,128)} %gain_hbm.1, ...), custom_call_target="tpu_custom_call" | custom-call | flops 7247757312 | bytes 16000000 | tf_op jit(solution)/shard_map/pallas_call | solution.py:494
  72.1 2.6 %shard_map.130 = (bf16[512,4608]{1,0:T(8,128)(2,1)}, bf16[512,512]{1,0:T(8,128)(2,1)}, f32[8,64,64]{2,1,0:T(8,128)}, f32[8,64,64]{2,1,0:T(8,128)}) custom-call(bf16[512,4608]{1,0:T(8,128)(2,1)S(1)} %get-tuple-element.12.refs_0_, bf16[512,512]{1,0:T(8,128)(2,1)S(1)} %get-tuple-element.13.refs_1_, f32[8,64,64]{2,1,0:T(8,128)S(1)} %get-tuple-element.14.refs_2_, ...), custom_call_target="tpu_custom_call" | custom-call | tf_op jit(solution)/shard_map/pallas_call | solution.py:539

commit v4 on v3

--- a/solution.py
+++ b/solution.py
@@ -36,7 +36,7 @@
     ids, keys, table,
     in_sem, w_sem, attn_sem,
     core_s, core_r, z_s, z_r, gz_s, gz_r, gc_s, gc_r, gf_s, gf_r,
-    pa_s, pa_r, pb_s, pb_r,
+    pa_s, pa_r, pb_s, pb_r, ready, go,
 ):
     n_rep = lax.axis_size("rep")
     planes = PLANES
@@ -99,14 +99,45 @@
     ids_load.start()
 
     barrier = pltpu.get_barrier_semaphore()
-    for rep_to, tp_to in (
-        (rep, sib), (rep, far), (plane_peer(near), tp), (plane_peer(next_near), tp)
-    ):
-        pl.semaphore_signal(barrier, inc=1, device_id=(rep_to, tp_to), device_id_type=MESH)
-
-    @pl.loop(1, n_xy)
-    def _(d):
-        pl.semaphore_signal(barrier, inc=1, device_id=(xy_peer(d), tp), device_id_type=MESH)
+    middle = (tp == 1) | (tp == 2)
+
+    @pl.when(jnp.logical_not(middle))
+    def _():
+        for to in (sib, far):
+            pl.semaphore_signal(barrier, inc=1, device_id=(rep, to), device_id_type=MESH)
+
+    @pl.when(middle)
+    def _():
+        pl.semaphore_wait(barrier, 2)
+        for to in (sib, far):
+            pl.semaphore_signal(ready, inc=1, device_id=(rep, to), device_id_type=MESH)
+
+    def greet_replicas():
+        @pl.when(jnp.logical_not(middle))
+        def _():
+            pl.semaphore_wait(ready, 2)
+
+        @pl.when(tp == 0)
+        def _():
+            for z in (near, next_near):
+                pl.semaphore_signal(
+                    barrier, inc=1, device_id=(plane_peer(z), 0), device_id_type=MESH
+                )
+
+            @pl.loop(1, n_xy)
+            def _(d):
+                pl.semaphore_signal(barrier, inc=1, device_id=(xy_peer(d), 0), device_id_type=MESH)
+
+    def meet_replicas():
+        @pl.when(tp == 0)
+        def _():
+            pl.semaphore_wait(barrier, n_xy + 1)
+            for to in range(1, PARTS):
+                pl.semaphore_signal(go, inc=1, device_id=(rep, to), device_id_type=MESH)
+
+        @pl.when(tp != 0)
+        def _():
+            pl.semaphore_wait(go, 1)
 
     def remote(src, dst, send, recv, rep_to, tp_to):
         return pltpu.make_async_remote_copy(
@@ -377,7 +408,7 @@
             copy.wait()
         if h == 0:
             w_load(0).wait()
-            pl.semaphore_wait(barrier, n_xy + 3)
+            greet_replicas()
         partial_tile(h, 0)
         if h == 0:
             for copy in others[1:]:
@@ -395,9 +426,10 @@
                 w_load(n).wait()
             partial_tile(h, n)
             pair_tile(h, n - 1)
-            if h == 0:
+            if h == HALVES - 1:
                 @pl.when(n == 1)
                 def _():
+                    meet_replicas()
                     table_copy().wait()
                     coef_load.wait()
 
@@ -410,14 +442,15 @@
     gain_load.wait()
     norm_half(0)
     send_far(0, 0, window)
+    norm_half(1)
+    use_half(0, 0, n_w - 4)
     sum_packs()
-    norm_half(1)
-    use_half(0, 0, window)
+    use_half(0, n_w - 4, n_w)
+    finish_input(0)
     pass_on()
-    use_half(0, window, n_w)
-    finish_input(0)
+    use_half(1, 0, n_w - 3)
     outer_step()
-    use_half(1, 0, n_w)
+    use_half(1, n_w - 3, n_w)
     finish_input(1)
 
     for h in range(HALVES):
@@ -528,6 +561,7 @@
             dma((9,)), dma((n_w,)), dma((HALVES * PARTS,)),
             *[dma((HALVES * n_w,)) for _ in range(10)],
             dma((n_xy,)), dma((n_xy,)), dma((2,)), dma((2,)),
+            pltpu.SemaphoreType.REGULAR, pltpu.SemaphoreType.REGULAR,
         ],
         compiler_params=pltpu.CompilerParams(
             collective_id=0, has_side_effects=True, vmem_limit_bytes=STEP_VMEM

time: 74.8 us -> 72.3 us (0.967)
  Pallas kernels: 74.1 us -> 71.5 us
    pallas_call x1, Pallas kernels: 71.5 us -> 69 us  [shards(): pl.pallas_call(step_kernel, out_shape=tuple((pltpu.VMEM(shape, dtype) for...]
where the time goes in v4:
time: 72.3 us; the launch traced here: 72.2 us
  Pallas kernels  71.5 us (99%)
    pallas_call x1, Pallas kernels, shards(): pl.pallas_call(step_kernel, out_shape=tuple((pltpu.VMEM(shape, dtype) for...  69 us
    pallas_call x1, Pallas kernels, shards(): pl.pallas_call(write_kernel, out_shape=tuple((jax.ShapeDtypeStruct(shape,...  2.59 us

profile of v4, /device:TPU:1, one launch (start us, length us, event | category | flops | bytes accessed | tf_op | source)
XLA Modules:
  0.0 72.2 jit_solution(9185898698495374999)
XLA Ops:
  0.6 69.0 %shard_map.129 = (bf16[512,4608]{1,0:T(8,128)(2,1)S(1)}, bf16[512,512]{1,0:T(8,128)(2,1)S(1)}, f32[8,64,64]{2,1,0:T(8,128)S(1)}, f32[8,64,64]{2,1,0:T(8,128)S(1)}) custom-call(s32[1,48]{1,0:T(1,128)} %bitcast.21, bf16[512,512]{1,0:T(8,128)(2,1)} %bitcast.15, bf16[512,4608]{1,0:T(8,128)(2,1)} %bitcast.11, f32[1,4608]{1,0:T(1,128)} %gain_hbm.1, ...), custom_call_target="tpu_custom_call" | custom-call | flops 7247757312 | bytes 16000000 | tf_op jit(solution)/shard_map/pallas_call | solution.py:527
  69.6 2.6 %shard_map.130 = (bf16[512,4608]{1,0:T(8,128)(2,1)}, bf16[512,512]{1,0:T(8,128)(2,1)}, f32[8,64,64]{2,1,0:T(8,128)}, f32[8,64,64]{2,1,0:T(8,128)}) custom-call(bf16[512,4608]{1,0:T(8,128)(2,1)S(1)} %get-tuple-element.12.refs_0_, bf16[512,512]{1,0:T(8,128)(2,1)S(1)} %get-tuple-element.13.refs_1_, f32[8,64,64]{2,1,0:T(8,128)S(1)} %get-tuple-element.14.refs_2_, ...), custom_call_target="tpu_custom_call" | custom-call | tf_op jit(solution)/shard_map/pallas_call | solution.py:573

commit v5 on v4

--- a/solution.py
+++ b/solution.py
@@ -14,6 +14,7 @@
 PARTS = 4
 HALVES = 2
 WINDOW = 5
+EARLY = 3
 AHEAD = 3
 STEP_VMEM = 55 * 1024 * 1024
 WRITE_FROM = pl.ANY
@@ -197,7 +198,6 @@
         part[here, cols(n)] = jnp.dot(
             attn[here, :], w[:, cols(n)], preferred_element_type=f32
         ).astype(bf16)
-        core_copy(h, n).start()
 
     def pair_tile(h, n):
         core_copy(h, n).wait_recv()
@@ -308,47 +308,69 @@
     half = lax.broadcasted_iota(jnp.int32, (1, 2 * side), 1)
     half = jnp.where(half < side, 0.0, 1.0).astype(f32)
 
-    def near_copy():
-        return remote(near_out, near_in, pb_s.at[0], pb_r.at[0], plane_peer(near), tp)
-
-    def last_copy():
-        return remote(last_out, last_in, pb_s.at[1], pb_r.at[1], plane_peer(next_near), tp)
+    def near_copies(slot):
+        return [
+            remote(
+                near_out.at[slot, pl.ds(p * side, side)], near_in.at[slot, pl.ds(p * side, side)],
+                pb_s.at[slot * pairs + p], pb_r.at[slot * pairs + p], plane_peer(near), tp,
+            )
+            for p in range(pairs)
+        ]
+
+    def last_copies():
+        return [
+            remote(
+                last_out.at[pl.ds(p * side, side)], last_in.at[pl.ds(p * side, side)],
+                pb_s.at[2 * pairs + p], pb_r.at[2 * pairs + p], plane_peer(next_near), tp,
+            )
+            for p in range(pairs)
+        ]
+
+    def sum_plane(z):
+        here_rows = pl.ds(pl.multiple_of(z * side, side), side)
+
+        def add(d, totals):
+            block = packs_in[d, here_rows, :].astype(f32)
+            turned = pltpu.roll(block, side, 1)
+            head = packs_in[d, planes * side:planes * side + HEAD, :].astype(f32)
+            head = jnp.sum(jnp.where(line == z, head, 0.0), axis=0, keepdims=True)
+            here = head - half
+            there = pltpu.roll(jnp.broadcast_to(head, (8, 2 * side)), side, 1)[0:1, :] - half
+            return tuple(
+                total
+                + jnp.where(here == 2.0 * p, block, 0.0)
+                + jnp.where(there == 2.0 * p, turned, 0.0)
+                for p, total in enumerate(totals)
+            )
+
+        zero = jnp.zeros((side, 2 * side), f32)
+        return lax.fori_loop(0, n_xy, add, (zero,) * pairs)
 
     def sum_packs():
         @pl.loop(1, n_xy)
         def _(d):
             pack_copy(d).wait_recv()
 
-        for h in range(planes):
-            def add(d, totals):
-                block = packs_in[d, h * side:(h + 1) * side, :].astype(f32)
-                turned = pltpu.roll(block, side, 1)
-                head = packs_in[d, planes * side:planes * side + HEAD, :].astype(f32)[h:h + 1, :]
-                here = head - half
-                there = pltpu.roll(jnp.broadcast_to(head, (8, 2 * side)), side, 1)[0:1, :] - half
-                return tuple(
-                    total
-                    + jnp.where(here == 2.0 * p, block, 0.0)
-                    + jnp.where(there == 2.0 * p, turned, 0.0)
-                    for p, total in enumerate(totals)
-                )
-
-            zero = jnp.zeros((side, 2 * side), f32)
-            totals = lax.fori_loop(0, n_xy, add, (zero,) * pairs)
-            for p in range(pairs):
-                sums[h, p * side:(p + 1) * side, :] = totals[p]
-        near_out[0] = sums[near].astype(bf16)
-        near_out[1] = sums[planes - 1 - near].astype(bf16)
-        near_copy().start()
+        for slot, z in ((1, planes - 1 - near), (0, near)):
+            for p, total in enumerate(sum_plane(z)):
+                near_out[slot, p * side:(p + 1) * side, :] = total.astype(bf16)
+            for copy in near_copies(slot):
+                copy.start()
+        for slot, z in ((1, next_near), (0, zh)):
+            for p, total in enumerate(sum_plane(z)):
+                sums[slot, p * side:(p + 1) * side, :] = total
 
     def pass_on():
-        near_copy().wait_recv()
-        last_out[...] = (sums[next_near] + near_in[1].astype(f32)).astype(bf16)
-        last_copy().start()
+        for copy in near_copies(1):
+            copy.wait_recv()
+        last_out[...] = (sums[1] + near_in[1].astype(f32)).astype(bf16)
+        for copy in last_copies():
+            copy.start()
 
     def outer_step():
-        last_copy().wait_recv()
-        total = sums[zh] + near_in[0].astype(f32) + last_in[...].astype(f32)
+        for copy in near_copies(0) + last_copies():
+            copy.wait_recv()
+        total = sums[0] + near_in[0].astype(f32) + last_in[...].astype(f32)
         for copy in (tiles_load, mom_load, left_load, right_load):
             copy.wait()
         wide = jnp.dot(total, right[...], precision=lax.Precision.HIGHEST)
@@ -408,8 +430,10 @@
             copy.wait()
         if h == 0:
             w_load(0).wait()
+        partial_tile(h, 0)
+        if h == 0:
             greet_replicas()
-        partial_tile(h, 0)
+        core_copy(h, 0).start()
         if h == 0:
             for copy in others[1:]:
                 copy.start()
@@ -425,6 +449,7 @@
 
                 w_load(n).wait()
             partial_tile(h, n)
+            core_copy(h, n).start()
             pair_tile(h, n - 1)
             if h == HALVES - 1:
                 @pl.when(n == 1)
@@ -443,9 +468,9 @@
     norm_half(0)
     send_far(0, 0, window)
     norm_half(1)
-    use_half(0, 0, n_w - 4)
+    use_half(0, 0, EARLY)
     sum_packs()
-    use_half(0, n_w - 4, n_w)
+    use_half(0, EARLY, n_w)
     finish_input(0)
     pass_on()
     use_half(1, 0, n_w - 3)
@@ -468,8 +493,8 @@
     def _(d):
         pack_copy(d).wait_send()
 
-    near_copy().wait_send()
-    last_copy().wait_send()
+    for copy in near_copies(0) + near_copies(1) + last_copies():
+        copy.wait_send()
 
 
 def write_kernel(*refs):
@@ -550,7 +575,7 @@
             pltpu.VMEM((tokens, depth), f32),
             pltpu.VMEM((n_xy, message, 2 * side), bf16),
             pltpu.VMEM((n_xy, message, 2 * side), bf16),
-            pltpu.VMEM((PLANES, summed, 2 * side), f32),
+            pltpu.VMEM((2, summed, 2 * side), f32),
             pltpu.VMEM((2, summed, 2 * side), bf16),
             pltpu.VMEM((2, summed, 2 * side), bf16),
             pltpu.VMEM((summed, 2 * side), bf16),
@@ -560,7 +585,7 @@
             pltpu.SMEM((n_rep, 128), jnp.int32),
             dma((9,)), dma((n_w,)), dma((HALVES * PARTS,)),
             *[dma((HALVES * n_w,)) for _ in range(10)],
-            dma((n_xy,)), dma((n_xy,)), dma((2,)), dma((2,)),
+            dma((n_xy,)), dma((n_xy,)), dma((3 * (owned // 2),)), dma((3 * (owned // 2),)),
             pltpu.SemaphoreType.REGULAR, pltpu.SemaphoreType.REGULAR,
         ],
         compiler_params=pltpu.CompilerParams(

time: 72.3 us -> 70 us (0.968)
  Pallas kernels: 71.5 us -> 69.2 us
    pallas_call x1, Pallas kernels: 69 us -> 66.7 us  [shards(): pl.pallas_call(step_kernel, out_shape=tuple((pltpu.VMEM(shape, dtype) for...]
where the time goes in v5:
time: 70 us; the launch traced here: 69.9 us
  Pallas kernels  69.2 us (99%)
    pallas_call x1, Pallas kernels, shards(): pl.pallas_call(step_kernel, out_shape=tuple((pltpu.VMEM(shape, dtype) for...  66.7 us
    pallas_call x1, Pallas kernels, shards(): pl.pallas_call(write_kernel, out_shape=tuple((jax.ShapeDtypeStruct(shape,...  2.59 us

profile of v5, /device:TPU:1, one launch (start us, length us, event | category | flops | bytes accessed | tf_op | source)
XLA Modules:
  0.0 69.9 jit_solution(1999532642253196296)
XLA Ops:
  0.6 66.7 %shard_map.129 = (bf16[512,4608]{1,0:T(8,128)(2,1)S(1)}, bf16[512,512]{1,0:T(8,128)(2,1)S(1)}, f32[8,64,64]{2,1,0:T(8,128)S(1)}, f32[8,64,64]{2,1,0:T(8,128)S(1)}) custom-call(s32[1,48]{1,0:T(1,128)} %bitcast.21, bf16[512,512]{1,0:T(8,128)(2,1)} %bitcast.15, bf16[512,4608]{1,0:T(8,128)(2,1)} %bitcast.11, f32[1,4608]{1,0:T(1,128)} %gain_hbm.1, ...), custom_call_target="tpu_custom_call" | custom-call | flops 7247757312 | bytes 16000000 | tf_op jit(solution)/shard_map/pallas_call | solution.py:552
  67.3 2.6 %shard_map.130 = (bf16[512,4608]{1,0:T(8,128)(2,1)}, bf16[512,512]{1,0:T(8,128)(2,1)}, f32[8,64,64]{2,1,0:T(8,128)}, f32[8,64,64]{2,1,0:T(8,128)}) custom-call(bf16[512,4608]{1,0:T(8,128)(2,1)S(1)} %get-tuple-element.12.refs_0_, bf16[512,512]{1,0:T(8,128)(2,1)S(1)} %get-tuple-element.13.refs_1_, f32[8,64,64]{2,1,0:T(8,128)S(1)} %get-tuple-element.14.refs_2_, ...), custom_call_target="tpu_custom_call" | custom-call | tf_op jit(solution)/shard_map/pallas_call | solution.py:598

commit v6 on v5

--- a/solution.py
+++ b/solution.py
@@ -13,7 +13,11 @@
 PLANES = 4
 PARTS = 4
 HALVES = 2
-WINDOW = 5
+WINDOW = 7
+GATHER = 5
+PACK_FROM = 5
+PIECES = 8
+LATE = 3
 EARLY = 3
 AHEAD = 3
 STEP_VMEM = 55 * 1024 * 1024
@@ -220,14 +224,14 @@
                 step(h - 1, n + n_w - window)
 
     def ahead(h, n, step):
-        @pl.when(n + window < n_w)
+        @pl.when(n + gather < n_w)
         def _():
-            step(h, n + window)
+            step(h, n + gather)
 
         if h < HALVES - 1:
-            @pl.when(n + window >= n_w)
+            @pl.when(n + gather >= n_w)
             def _():
-                step(h + 1, n + window - n_w)
+                step(h + 1, n + gather - n_w)
 
     def fold(block):
         total = block[:, 0:128]
@@ -294,7 +298,7 @@
 
     def pack_some(n):
         for i in range(each):
-            d = (n - 1) * each + 1 + i
+            d = n * each + 1 + i
 
             @pl.when(d < n_xy)
             def _():
@@ -424,7 +428,8 @@
             base = (h * PARTS + p) * s
             ig[pl.ds(start, s), :] = ig_acc[base:base + s, :].astype(bf16)
 
-    window = min(WINDOW, n_w)
+    window, gather = min(WINDOW, n_w), min(GATHER, n_w)
+    pack_from = min(PACK_FROM, n_w - 1)
     for h in range(HALVES):
         for copy in loads[h * PARTS:(h + 1) * PARTS]:
             copy.wait()
@@ -439,6 +444,7 @@
                 copy.start()
             ids_load.wait()
             make_table()
+            pair_tile(0, 0)
 
         @pl.loop(1, n_w)
         def _(n):
@@ -450,15 +456,24 @@
                 w_load(n).wait()
             partial_tile(h, n)
             core_copy(h, n).start()
-            pair_tile(h, n - 1)
-            if h == HALVES - 1:
-                @pl.when(n == 1)
+            if h == 0:
+                @pl.when(n > 1)
                 def _():
-                    meet_replicas()
+                    pair_tile(h, n - 1)
+
+                @pl.when(n == pack_from)
+                def _():
                     table_copy().wait()
                     coef_load.wait()
-
-                pack_some(n)
+                    meet_replicas()
+
+                @pl.when(n >= pack_from)
+                def _():
+                    pack_some(n - pack_from)
+            else:
+                pair_tile(h, n - 1)
+                if h == 1:
+                    pack_some(n + n_w - 1 - pack_from)
 
         pair_tile(h, n_w - 1)
     attn_t[...] = attn[...].T
@@ -466,23 +481,25 @@
     ct_load.wait()
     gain_load.wait()
     norm_half(0)
-    send_far(0, 0, window)
+    send_far(0, 0, gather)
     norm_half(1)
     use_half(0, 0, EARLY)
     sum_packs()
     use_half(0, EARLY, n_w)
     finish_input(0)
     pass_on()
-    use_half(1, 0, n_w - 3)
+    use_half(1, 0, n_w - LATE)
     outer_step()
-    use_half(1, n_w - 3, n_w)
-    finish_input(1)
-
+    last = n_w - LATE
     for h in range(HALVES):
         @pl.loop(0, n_w)
         def _(n):
             core_copy(h, n).wait_send()
             grad_core(h, n).wait_send()
+
+    for h in range(HALVES):
+        @pl.loop(0, n_w if h < HALVES - 1 else last)
+        def _(n):
             grad_forward(h, n).wait_send()
 
     @pl.loop(n_w - window, n_w)
@@ -495,11 +512,17 @@
 
     for copy in near_copies(0) + near_copies(1) + last_copies():
         copy.wait_send()
+    use_half(1, last, n_w)
+    finish_input(1)
+
+    @pl.loop(last, n_w)
+    def _(n):
+        grad_forward(HALVES - 1, n).wait_send()
 
 
 def write_kernel(*refs):
     sources, targets, sem = refs[:4], refs[4:8], refs[8]
-    pieces = 8
+    pieces = PIECES
     step = sources[0].shape[0] // pieces
     copies = [
         pltpu.make_async_copy(
@@ -600,7 +623,7 @@
         out_shape=tuple(jax.ShapeDtypeStruct(shape, dtype) for shape, dtype in results),
         in_specs=[pl.BlockSpec(memory_space=WRITE_FROM)] * 4,
         out_specs=(any_spec,) * 4,
-        scratch_shapes=[dma((11,))],
+        scratch_shapes=[dma((PIECES + 3,))],
         compiler_params=pltpu.CompilerParams(vmem_limit_bytes=4 * 1024 * 1024),
     )(*held)
     return tuple(out[None] for out in outs)

time: 70 us -> 70.2 us (level)
  no operation moved by 1% of the time
where the time goes in v6:
time: 70.2 us; the launch traced here: 70 us
  Pallas kernels  69.4 us (99%)
    pallas_call x1, Pallas kernels, shards(): pl.pallas_call(step_kernel, out_shape=tuple((pltpu.VMEM(shape, dtype) for...  66.8 us
    pallas_call x1, Pallas kernels, shards(): pl.pallas_call(write_kernel, out_shape=tuple((jax.ShapeDtypeStruct(shape,...  2.59 us

profile of v6, /device:TPU:1, one launch (start us, length us, event | category | flops | bytes accessed | tf_op | source)
XLA Modules:
  0.0 70.0 jit_solution(18367972921782841604)
XLA Ops:
  0.6 66.8 %shard_map.129 = (bf16[512,4608]{1,0:T(8,128)(2,1)S(1)}, bf16[512,512]{1,0:T(8,128)(2,1)S(1)}, f32[8,64,64]{2,1,0:T(8,128)S(1)}, f32[8,64,64]{2,1,0:T(8,128)S(1)}) custom-call(s32[1,48]{1,0:T(1,128)} %bitcast.21, bf16[512,512]{1,0:T(8,128)(2,1)} %bitcast.15, bf16[512,4608]{1,0:T(8,128)(2,1)} %bitcast.11, f32[1,4608]{1,0:T(1,128)} %gain_hbm.1, ...), custom_call_target="tpu_custom_call" | custom-call | flops 7247757312 | bytes 16000000 | tf_op jit(solution)/shard_map/pallas_call | solution.py:575
  67.4 2.6 %shard_map.130 = (bf16[512,4608]{1,0:T(8,128)(2,1)}, bf16[512,512]{1,0:T(8,128)(2,1)}, f32[8,64,64]{2,1,0:T(8,128)}, f32[8,64,64]{2,1,0:T(8,128)}) custom-call(bf16[512,4608]{1,0:T(8,128)(2,1)S(1)} %get-tuple-element.12.refs_0_, bf16[512,512]{1,0:T(8,128)(2,1)S(1)} %get-tuple-element.13.refs_1_, f32[8,64,64]{2,1,0:T(8,128)S(1)} %get-tuple-element.14.refs_2_, ...), custom_call_target="tpu_custom_call" | custom-call | tf_op jit(solution)/shard_map/pallas_call | solution.py:621
